TPU v7x, 256 devices: a whole 4x4x8 slice. The times are simulated.
256 devices in a mesh: scene: 4 (over x), dom: 64 (over z, y, core).
Axes of the slice: x: 4, y: 4, z: 8, core: 2. Of those that a mesh axis runs over, the one named last changes fastest.
Arguments:
- features: bfloat16 [2048, 64, 512], P(('scene', 'dom')), parts along dimension 0, may hold values from -6 to 6
- cotangent: bfloat16 [2048, 64, 512], P(('scene', 'dom')), parts along dimension 0, may hold values from -6 to 6
- weight: bfloat16 [27, 64, 64], replicated, may hold values from -0.15625 to 0.15625
- mask_words: int32 [2048, 18], P(('scene', 'dom')), parts along dimension 0, may hold values from 0 to 1073741823, as said below
- neighbors: int32 [2048, 26], P(('scene', 'dom')), parts along dimension 0, may hold values from -1 to 511, as said below
Outputs:
- out_features: bfloat16 [2048, 64, 512], P(('scene', 'dom')), parts along dimension 0
- in_grad: bfloat16 [2048, 64, 512], P(('scene', 'dom')), parts along dimension 0
- weight_grad: float32 [108, 64, 64], P('scene'), parts along dimension 0
There are 4 independent parts, one for each index of `scene`. A program takes and returns all parts, laid end to end along the dimension named above; an argument that names none is the same for every part. Nothing has to cross between parts.
Inputs may be any that keep to these rules, and one draw needn't show every extreme that they name: `mask_words`: bit r of word w is voxel 30 w + r of the leaf; bits at or past 512 are 0; unused slots have all bits 0. An id is owner * 8 + slot, owner being the index along dom. All leaves at one leaf position along the first dimension have the same owner; a neighbor at first offset -1 is owned by the same device or the one below it, at +1 by the same device or the one above it. The table is symmetric: b is listed as a neighbor of a at offset (p, q, r) exactly when a is listed for b at (-p, -q, -r). Used slots of a device come first; unused slots list no neighbors. At most 4 leaves of one device have a neighbor owned by one given adjacent device, and some device reaches that in every draw; some device uses all 8 slots in every draw.
All inputs are finite; a program needn't handle non-finite values.
Results may differ from a plain program's by a relative error of at most 0.001.
Values may be sent and summed in bfloat16 or wider, within the bound.
A program may use at most 256 MiB of HBM per device.

v0:
```python
import jax
import jax.numpy as jnp
import numpy as np
from jax import lax
from jax.sharding import PartitionSpec as P

LEAF = 8


def with_halo(shard, sides, width):
    for axis, dim in sides:
        size, length = (lax.axis_size(axis), shard.shape[dim])
        up = [(i, (i + 1) % size) for i in range(size - 1)]
        down = [(j, i) for i, j in up]
        last = lax.slice_in_dim(shard, length - width, length, axis=dim)
        leading = lax.slice_in_dim(shard, 0, width, axis=dim)
        before = lax.ppermute(last, axis, up)
        after = lax.ppermute(leading, axis, down)
        shard = jnp.concatenate([before, shard, after], axis=dim)
    return shard


def unpack_voxels(mask_words, voxel_count):
    bit_place = jnp.arange(30, dtype=jnp.int32)
    bit_values = jnp.right_shift(mask_words[:, :, None], bit_place[None, None, :]) & 1
    return bit_values.reshape(mask_words.shape[0], -1)[:, :voxel_count]


def column_of(shift_x, shift_y, shift_z):
    tap_number = (shift_x + 1) * 9 + (shift_y + 1) * 3 + shift_z + 1
    return tap_number if tap_number < 13 else tap_number - 1


def tap_offsets():
    return [
        (shift_x, shift_y, shift_z)
        for shift_x in (-1, 0, 1)
        for shift_y in (-1, 0, 1)
        for shift_z in (-1, 0, 1)
    ]


def axis_cells(shift_value, extent):
    if shift_value < 0:
        return ([0], [extent - 1])
    if shift_value > 0:
        return ([extent + 1], [0])
    return (list(range(1, extent + 1)), list(range(extent)))


def region_tables(offset, extent):
    side = extent + 2
    dest_a, src_a = axis_cells(offset[0], extent)
    dest_b, src_b = axis_cells(offset[1], extent)
    dest_c, src_c = axis_cells(offset[2], extent)
    dest_list = []
    src_list = []
    for index_a in range(len(dest_a)):
        for index_b in range(len(dest_b)):
            for index_c in range(len(dest_c)):
                dest_list.append(
                    (dest_a[index_a] * side + dest_b[index_b]) * side + dest_c[index_c]
                )
                if offset[0] == 0:
                    src_list.append(
                        (src_a[index_a] * extent + src_b[index_b]) * extent + src_c[index_c]
                    )
                else:
                    src_list.append(src_b[index_b] * extent + src_c[index_c])
    return (np.array(dest_list, dtype=np.int32), np.array(src_list, dtype=np.int32))


def take_rows(source, row_index, keep_rows):
    picked = jnp.take(source, jnp.clip(row_index, 0, source.shape[0] - 1), axis=0)
    return jnp.where(keep_rows[:, None, None], picked, jnp.zeros((), source.dtype))


def shards(features, cotangent, weight, mask_words, neighbors):
    leaf_count, channels, voxel_count = features.shape
    edge_cells = LEAF
    side = edge_cells + 2
    padded_cells = side**3
    span_start = side * side + side + 1
    span_cells = padded_cells - 2 * span_start
    face_cells = edge_cells * edge_cells
    device = lax.axis_index("dom")
    occupancy = unpack_voxels(mask_words, voxel_count).astype(features.dtype)
    masked_x = features * occupancy[:, None, :]
    masked_dy = cotangent * occupancy[:, None, :]
    plane_size = channels * face_cells
    low_planes = jnp.stack(
        [
            masked_x[:, :, :face_cells].reshape(leaf_count, plane_size),
            masked_dy[:, :, :face_cells].reshape(leaf_count, plane_size),
        ]
    )
    high_planes = jnp.stack(
        [
            masked_x[:, :, voxel_count - face_cells :].reshape(leaf_count, plane_size),
            masked_dy[:, :, voxel_count - face_cells :].reshape(leaf_count, plane_size),
        ]
    )
    present = neighbors >= 0
    owner_dev = jnp.where(present, neighbors // leaf_count, -2)
    local_here = present & (owner_dev == device)
    from_below = present & (owner_dev == device - 1)
    from_above = present & (owner_dev == device + 1)
    slot_here = neighbors - device * leaf_count
    slot_below = neighbors - (device - 1) * leaf_count
    slot_above = neighbors - (device + 1) * leaf_count
    outgoing = jnp.stack([low_planes, high_planes])
    received = with_halo(outgoing, (("dom", 0),), 1)
    offsets = tap_offsets()
    inner_dest, inner_src = region_tables((0, 0, 0), edge_cells)

    def padded_field(field_number, center):
        pool_high = jnp.concatenate(
            [high_planes[field_number], received[0, field_number]], axis=0
        ).reshape(-1, channels, face_cells)
        pool_low = jnp.concatenate(
            [low_planes[field_number], received[3, field_number]], axis=0
        ).reshape(-1, channels, face_cells)
        padded = (
            jnp.zeros((leaf_count, channels, padded_cells), center.dtype)
            .at[:, :, inner_dest]
            .set(center)
        )
        for offset in offsets:
            if offset == (0, 0, 0):
                continue
            dest_index, src_index = region_tables(offset, edge_cells)
            column = column_of(offset[0], offset[1], offset[2])
            if offset[0] == 0:
                source = jnp.take(center, src_index, axis=2)
                row_index = slot_here[:, column]
                keep_rows = local_here[:, column]
            elif offset[0] < 0:
                source = jnp.take(pool_high, src_index, axis=2)
                row_index = jnp.where(
                    local_here[:, column], slot_here[:, column], leaf_count + slot_below[:, column]
                )
                keep_rows = local_here[:, column] | from_below[:, column]
            else:
                source = jnp.take(pool_low, src_index, axis=2)
                row_index = jnp.where(
                    local_here[:, column], slot_here[:, column], leaf_count + slot_above[:, column]
                )
                keep_rows = local_here[:, column] | from_above[:, column]
            padded = padded.at[:, :, dest_index].set(take_rows(source, row_index, keep_rows))
        return padded

    padded_x = padded_field(0, masked_x)
    padded_dy = padded_field(1, masked_dy)
    span_dy = (
        jnp.zeros((leaf_count, channels, span_cells), masked_dy.dtype)
        .at[:, :, inner_dest - span_start]
        .set(masked_dy)
    )
    shift_list = [(offset[0] * side + offset[1]) * side + offset[2] for offset in offsets]
    group_size = max(1, leaf_count // 8)
    block_count = leaf_count // group_size
    flat_weight = weight.reshape(27 * channels, channels)
    turned_weight = jnp.transpose(weight, (1, 0, 2)).reshape(channels, 27 * channels)

    def block_terms(inputs):
        pad_x_block, pad_dy_block, dy_block = inputs
        stack_x = jnp.concatenate(
            [
                pad_x_block[:, :, span_start + shift : span_start + shift + span_cells]
                for shift in shift_list
            ],
            axis=1,
        )
        stack_dy = jnp.concatenate(
            [
                pad_dy_block[:, :, span_start - shift : span_start - shift + span_cells]
                for shift in shift_list
            ],
            axis=1,
        )
        out_block = jnp.einsum(
            "ko,lkv->lov", flat_weight, stack_x, preferred_element_type=jnp.float32
        )
        back_block = jnp.einsum(
            "ik,lkv->liv", turned_weight, stack_dy, preferred_element_type=jnp.float32
        )
        grad_block = jnp.einsum(
            "lkv,lov->ko", stack_x, dy_block, preferred_element_type=jnp.float32
        )
        return (out_block, back_block, grad_block)

    def regroup(array):
        return array.reshape((block_count, group_size) + array.shape[1:])

    out_parts, back_parts, grad_parts = lax.map(
        block_terms, (regroup(padded_x), regroup(padded_dy), regroup(span_dy))
    )
    out_sum = out_parts.reshape(leaf_count, channels, span_cells)
    back_sum = back_parts.reshape(leaf_count, channels, span_cells)
    grad_local = jnp.sum(grad_parts, axis=0).reshape(27, channels, channels)
    inner_span = inner_dest - span_start
    occupancy_wide = occupancy.astype(jnp.float32)[:, None, :]
    out_features = (jnp.take(out_sum, inner_span, axis=2) * occupancy_wide).astype(jnp.bfloat16)
    in_grad = (jnp.take(back_sum, inner_span, axis=2) * occupancy_wide).astype(jnp.bfloat16)
    grad_scale = float(lax.axis_size("dom") * leaf_count * voxel_count) ** (-0.5)
    summed_grad = lax.psum(grad_local.reshape(-1), "dom")
    weight_grad = summed_grad.reshape(27, channels, channels) * grad_scale
    return (out_features, in_grad, weight_grad)


def solution(mesh):
    placed = (
        P(("scene", "dom"), None, None),
        P(("scene", "dom"), None, None),
        P(),
        P(("scene", "dom"), None),
        P(("scene", "dom"), None),
    )
    return jax.shard_map(
        shards,
        mesh=mesh,
        in_specs=placed,
        out_specs=(
            P(("scene", "dom"), None, None),
            P(("scene", "dom"), None, None),
            P("scene", None, None),
        ),
        check_vma=False,
    )
```

profile of v0, /device:TPU:1, one launch (start us, length us, event | category | flops | bytes accessed | tf_op | source)
XLA Modules:
  0.0 636.6 jit_solution(8888239255000274014)
XLA Ops:
  8.4 1.8 copy.271
  15.2 5.3 collective-permute-start.1
  21.9 1.9 collective-permute-start
  87.8 13.8 %scatter_fusion.38 = bf16[8,64,778]{1,0,2:T(8,128)(2,1)S(1)} fusion(bf16[8,64,778]{1,0,2:T(8,128)(2,1)S(1)} %broadcast_in_dim.665, s32[512]{0:T(512)} %constant.642.clone, bf16[512,8,64]{2,1,0:T(8,128)(2,1)S(1)} %bitcast.358), kind=kCustom, calls=%fused_computation.128 | custom fusion | bytes 1574912 | tf_op jit(solution)/shard_map/scatter | solution.py:157
  101.6 2.5 copy.356
  105.8 13.7 %scatter_fusion.19 = bf16[8,64,1000]{1,0,2:T(8,128)(2,1)S(1)} fusion(bf16[8,64,1000]{1,0,2:T(8,128)(2,1)S(1)} %broadcast.489.clone, s32[512]{0:T(512)} %constant.1068, bf16[512,8,64]{2,1,0:T(8,128)(2,1)S(1)} %bitcast.359), kind=kCustom, calls=%fused_computation.109 | custom fusion | bytes 1574912 | tf_op jit(solution)/shard_map/scatter | solution.py:126
  122.1 13.7 %scatter_fusion = bf16[8,64,1000]{1,0,2:T(8,128)(2,1)S(1)} fusion(bf16[8,64,1000]{1,0,2:T(8,128)(2,1)S(1)} %broadcast.489.clone.1, s32[512]{0:T(512)} %constant.1068, bf16[512,8,64]{2,1,0:T(8,128)(2,1)S(1)} %bitcast.361), kind=kCustom, calls=%fused_computation.90 | custom fusion | bytes 1574912 | tf_op jit(solution)/shard_map/scatter | solution.py:126
  176.0 1.9 gather_fusion
  177.9 2.0 gather_fusion.44
  182.0 1.9 gather_fusion.3
  183.9 1.9 gather_fusion.47
  188.7 2.2 select_bitcast_fusion
  195.5 1.8 fusion.34
  204.4 1.9 gather_fusion.10
  206.3 1.9 gather_fusion.54
  208.9 1.9 gather_fusion.13
  210.9 1.9 gather_fusion.57
  212.8 2.0 gather_fusion.30
  214.7 1.9 gather_fusion.74
  218.9 1.9 gather_fusion.33
  220.8 1.9 gather_fusion.77
  243.1 2.1 scatter_fusion.20
  247.4 2.1 scatter_fusion.21
  249.5 2.7 scatter_fusion.3
  252.2 6.5 %scatter_fusion.22 = bf16[8,64,1000]{1,0,2:T(8,128)(2,1)} fusion(bf16[8,64,1000]{1,0,2:T(8,128)(2,1)} %scatter_fusion.21, s32[64]{0:T(128)S(1)} %copy-done.81, bf16[64,8,64]{2,1,0:T(8,128)(2,1)S(1)} %copy-done.47), kind=kCustom, calls=%fused_computation.112 | custom fusion | bytes 196864 | tf_op jit(solution)/shard_map/scatter | solution.py:149
  259.5 1.9 scatter_fusion.23
  262.8 1.9 scatter_fusion.24
  266.2 1.9 scatter_fusion.25
  268.1 2.6 scatter_fusion.7
  270.7 6.9 %scatter_fusion.26 = bf16[8,64,1000]{1,0,2:T(8,128)(2,1)} fusion(bf16[8,64,1000]{1,0,2:T(8,128)(2,1)} %scatter_fusion.25, s32[64]{0:T(128)S(1)} %copy-done.77, bf16[64,8,64]{2,1,0:T(8,128)(2,1)} %copy.329), kind=kCustom, calls=%fused_computation.116 | custom fusion | bytes 196864 | tf_op jit(solution)/shard_map/scatter | solution.py:149
  278.3 1.9 scatter_fusion.27
  280.2 2.4 scatter_fusion.9
  282.7 6.9 %scatter_fusion.28 = bf16[8,64,1000]{1,0,2:T(8,128)(2,1)} fusion(bf16[8,64,1000]{1,0,2:T(8,128)(2,1)} %scatter_fusion.27, s32[64]{0:T(128)S(1)} %copy-done.75, bf16[64,8,64]{2,1,0:T(8,128)(2,1)} %copy.333), kind=kCustom, calls=%fused_computation.118 | custom fusion | bytes 196864 | tf_op jit(solution)/shard_map/scatter | solution.py:149
  289.6 2.4 scatter_fusion.10
  292.1 6.6 %scatter_fusion.29 = bf16[8,64,1000]{1,0,2:T(8,128)(2,1)} fusion(bf16[8,64,1000]{1,0,2:T(8,128)(2,1)} %scatter_fusion.28, s32[64]{0:T(128)S(1)} %copy-done.74, bf16[64,8,64]{2,1,0:T(8,128)(2,1)S(1)} %copy-done.44), kind=kCustom, calls=%fused_computation.119 | custom fusion | bytes 196864 | tf_op jit(solution)/shard_map/scatter | solution.py:149
  299.4 1.9 scatter_fusion.30
  301.3 2.4 scatter_fusion.12
  303.8 6.6 %scatter_fusion.31 = bf16[8,64,1000]{1,0,2:T(8,128)(2,1)} fusion(bf16[8,64,1000]{1,0,2:T(8,128)(2,1)} %scatter_fusion.30, s32[64]{0:T(128)S(1)} %copy-done.72, bf16[64,8,64]{2,1,0:T(8,128)(2,1)S(1)} %copy-done.42), kind=kCustom, calls=%fused_computation.121 | custom fusion | bytes 196864 | tf_op jit(solution)/shard_map/scatter | solution.py:149
  311.1 1.9 scatter_fusion.32
  314.4 1.9 scatter_fusion.33
  317.7 1.9 scatter_fusion.34
  319.6 2.4 scatter_fusion.16
  322.1 6.5 %scatter_fusion.35 = bf16[8,64,1000]{1,0,2:T(8,128)(2,1)} fusion(bf16[8,64,1000]{1,0,2:T(8,128)(2,1)} %scatter_fusion.34, s32[64]{0:T(128)S(1)} %copy-done.68, bf16[64,8,64]{2,1,0:T(8,128)(2,1)S(1)} %copy-done.46), kind=kCustom, calls=%fused_computation.125 | custom fusion | bytes 196864 | tf_op jit(solution)/shard_map/scatter | solution.py:149
  329.3 1.9 scatter_fusion.36
  332.6 1.9 scatter_fusion.37
  335.1 1.9 copy.354
  337.1 2.6 copy.355
  339.6 89.4 %while.31 = (s32[]{:T(128)}, f32[8,1,64,778]{3,2,1,0:T(8,128)}, f32[8,1,64,778]{3,2,1,0:T(8,128)}, f32[8,1728,64]{1,2,0:T(8,128)}, bf16[8,1,64,1000]{3,2,1,0:T(8...) while((s32[]{:T(128)}, f32[8,1,64,778]{3,2,1,0:T(8,128)}, ...), condition=%wide.region_56.67_spmd, body=%wide.region_55.66_spmd.sunk | while | flops 516243456 | bytes 22411112 | solution.py:195
  347.0 2.7 fusion.141
  358.2 2.7 fusion.141
  369.3 2.7 fusion.141
  380.4 2.7 fusion.141
  391.5 2.7 fusion.141
  402.7 2.7 fusion.141
  413.8 2.7 fusion.141
  425.0 2.7 fusion.141
  429.0 3.6 copy.357
  432.6 2.8 copy.359
  435.4 4.2 gather_fusion.88
  439.6 2.7 gather_fusion.89
  442.3 2.3 reduce_sum.9
  446.4 2.8 fusion.27
  449.1 2.6 copy.361
  453.3 174.1 %all-reduce.2.cloned.1.call-done = f32[110592]{0:T(1024)} async-done(((f32[110592]{0:T(1024)}), f32[110592]{0:T(1024)}) %all-reduce.2.cloned.1.call-update) | async-done | bytes 442384 | tf_op jit(solution)/shard_map/psum | solution.py:206
  (1026 shorter events, 239.0 us)
Async XLA Ops:
  7.2 620.2 %all-reduce.2.cloned.1.call-start = ((), (), s32[]{:S(2)}) async-start(), calls=%async_computation | async-start | bytes 884736 | tf_op jit(solution)/shard_map/psum | solution.py:206
  13.7 28.5 %copy-start.3 = (bf16[8,64,512]{1,0,2:T(8,128)(2,1)}, bf16[8,64,512]{1,0,2:T(8,128)(2,1)S(1)}, u32[]{:S(2)}) copy-start(bf16[8,64,512]{1,0,2:T(8,128)(2,1)S(1)} %get-tuple-element.404) | copy-start | bytes 1572868
  15.2 23.5 %copy-start.114 = (s32[8]{0:T(128)S(1)}, s32[8]{0:T(128)}, u32[]{:S(2)}) copy-start(s32[8]{0:T(128)} %constant.1135) | copy-start | bytes 100
  15.2 133.5 %collective-permute-start.1 = (bf16[1,2,8,4096]{3,2,1,0:T(8,128)(2,1)}, bf16[1,2,8,4096]{3,2,1,0:T(8,128)(2,1)}, u32[]{:S(2)}, u32[]{:S(2)}) collective-permute-start(bf16[1,2,8,4096]{3,2,1,0:T(8,128)(2,1)} %maximum_bitcast_fusion.1), channel_id=1, source_target_pairs={{1,0},{2,1},{3,2},{4,3},{5,4},{6,5},{7,6},{8,7},{9,8},{10,9},{11,1... | collective-permute-start | bytes 393224 | tf_op jit(solution)/shard_map/ppermute | solution.py:18
  21.9 114.8 %collective-permute-start = (bf16[1,2,8,4096]{3,2,1,0:T(8,128)(2,1)}, bf16[1,2,8,4096]{3,2,1,0:T(8,128)(2,1)}, u32[]{:S(2)}, u32[]{:S(2)}) collective-permute-start(bf16[1,2,8,4096]{3,2,1,0:T(8,128)(2,1)} %maximum_bitcast_fusion), channel_id=1, source_target_pairs={{0,1},{1,2},{2,3},{3,4},{4,5},{5,6},{6,7},{7,8},{8,9},{9,10},{10,1... | collective-permute-start | bytes 393224 | tf_op jit(solution)/shard_map/ppermute | solution.py:17
  48.9 95.8 %copy-start.52 = (s32[1024]{0:T(1024)}, s32[1024]{0:T(1024)S(1)}, u32[]{:S(2)}) copy-start(s32[1024]{0:T(1024)S(1)} %pad_clamp_fusion.38) | copy-start | bytes 12292
  50.1 96.9 %copy-start.53 = (s32[1024]{0:T(1024)}, s32[1024]{0:T(1024)S(1)}, u32[]{:S(2)}) copy-start(s32[1024]{0:T(1024)S(1)} %pad_clamp_fusion.35) | copy-start | bytes 12292
  194.0 31.0 %copy-start.37 = (bf16[16,64,64]{1,0,2:T(8,128)(2,1)S(1)}, bf16[16,64,64]{1,0,2:T(8,128)(2,1)}, u32[]{:S(2)}) copy-start(bf16[16,64,64]{1,0,2:T(8,128)(2,1)} %get-tuple-element.472) | copy-start | bytes 393220
  195.5 30.5 %copy-start.36 = (bf16[16,64,64]{1,0,2:T(8,128)(2,1)S(1)}, bf16[16,64,64]{1,0,2:T(8,128)(2,1)}, u32[]{:S(2)}) copy-start(bf16[16,64,64]{1,0,2:T(8,128)(2,1)} %get-tuple-element.471) | copy-start | bytes 393220
  199.8 29.6 %copy-start.101 = (pred[8]{0:T(512)(128)(4,1)S(1)}, pred[8]{0:T(512)(128)(4,1)}, u32[]{:S(2)}) copy-start(pred[8]{0:T(512)(128)(4,1)} %get-tuple-element.335) | copy-start | bytes 28
  199.8 29.6 %copy-start.102 = (pred[8]{0:T(512)(128)(4,1)S(1)}, pred[8]{0:T(512)(128)(4,1)}, u32[]{:S(2)}) copy-start(pred[8]{0:T(512)(128)(4,1)} %get-tuple-element.511) | copy-start | bytes 28
  203.6 27.5 %copy-start.49 = (bf16[16,64,8]{1,0,2:T(8,128)(2,1)S(1)}, bf16[16,64,8]{1,0,2:T(8,128)(2,1)}, u32[]{:S(2)}) copy-start(bf16[16,64,8]{1,0,2:T(8,128)(2,1)} %get-tuple-element.468) | copy-start | bytes 49156
  231.9 26.8 %copy-start.80 = (s32[8]{0:T(128)S(1)}, s32[8]{0:T(128)}, u32[]{:S(2)}) copy-start(s32[8]{0:T(128)} %constant.1072) | copy-start | bytes 100
  235.0 26.4 %copy-start.64 = (bf16[8,64]{1,0:T(8,128)(2,1)S(1)}, bf16[8,64]{1,0:T(8,128)(2,1)}, u32[]{:S(2)}) copy-start(bf16[8,64]{1,0:T(8,128)(2,1)} %gather_fusion.10) | copy-start | bytes 3076
  235.0 26.4 %copy-start.65 = (bf16[8,64]{1,0:T(8,128)(2,1)S(1)}, bf16[8,64]{1,0:T(8,128)(2,1)}, u32[]{:S(2)}) copy-start(bf16[8,64]{1,0:T(8,128)(2,1)} %gather_fusion.54) | copy-start | bytes 3076
  235.0 26.4 %copy-start.93 = (pred[8]{0:T(512)(128)(4,1)S(1)}, pred[8]{0:T(512)(128)(4,1)}, u32[]{:S(2)}) copy-start(pred[8]{0:T(512)(128)(4,1)} %get-tuple-element.342) | copy-start | bytes 28
  235.0 26.4 %copy-start.97 = (pred[8]{0:T(512)(128)(4,1)S(1)}, pred[8]{0:T(512)(128)(4,1)}, u32[]{:S(2)}) copy-start(pred[8]{0:T(512)(128)(4,1)} %get-tuple-element.527) | copy-start | bytes 28
  235.0 27.1 %copy-start.79 = (s32[8]{0:T(128)S(1)}, s32[8]{0:T(128)}, u32[]{:S(2)}) copy-start(s32[8]{0:T(128)} %constant.1073) | copy-start | bytes 100
  238.5 26.2 %copy-start.62 = (bf16[8,64]{1,0:T(8,128)(2,1)S(1)}, bf16[8,64]{1,0:T(8,128)(2,1)}, u32[]{:S(2)}) copy-start(bf16[8,64]{1,0:T(8,128)(2,1)} %gather_fusion.13) | copy-start | bytes 3076
  238.6 26.2 %copy-start.63 = (bf16[8,64]{1,0:T(8,128)(2,1)S(1)}, bf16[8,64]{1,0:T(8,128)(2,1)}, u32[]{:S(2)}) copy-start(bf16[8,64]{1,0:T(8,128)(2,1)} %gather_fusion.57) | copy-start | bytes 3076
  238.6 26.1 %copy-start.92 = (pred[8]{0:T(512)(128)(4,1)S(1)}, pred[8]{0:T(512)(128)(4,1)}, u32[]{:S(2)}) copy-start(pred[8]{0:T(512)(128)(4,1)} %get-tuple-element.340) | copy-start | bytes 28
  238.6 26.1 %copy-start.94 = (pred[8]{0:T(512)(128)(4,1)S(1)}, pred[8]{0:T(512)(128)(4,1)}, u32[]{:S(2)}) copy-start(pred[8]{0:T(512)(128)(4,1)} %get-tuple-element.525) | copy-start | bytes 28
  238.6 26.8 %copy-start.30 = (bf16[8,8,64]{2,1,0:T(8,128)(2,1)S(1)}, bf16[8,8,64]{2,1,0:T(8,128)(2,1)}, u32[]{:S(2)}) copy-start(bf16[8,8,64]{2,1,0:T(8,128)(2,1)} %copy.287) | copy-start | bytes 24580
  238.6 26.8 %copy-start.78 = (s32[8]{0:T(128)S(1)}, s32[8]{0:T(128)}, u32[]{:S(2)}) copy-start(s32[8]{0:T(128)} %constant.1074) | copy-start | bytes 100
  242.1 24.1 %copy-start.32 = (bf16[8,8,64]{2,1,0:T(8,128)(2,1)S(1)}, bf16[8,8,64]{2,1,0:T(8,128)(2,1)}, u32[]{:S(2)}) copy-start(bf16[8,8,64]{2,1,0:T(8,128)(2,1)} %copy.327) | copy-start | bytes 24580
  243.0 25.0 %copy-start.43 = (bf16[64,8,64]{2,1,0:T(8,128)(2,1)S(1)}, bf16[64,8,64]{2,1,0:T(8,128)(2,1)}, u32[]{:S(2)}) copy-start(bf16[64,8,64]{2,1,0:T(8,128)(2,1)} %copy.289) | copy-start | bytes 196612
  243.1 25.0 %copy-start.77 = (s32[64]{0:T(128)S(1)}, s32[64]{0:T(128)}, u32[]{:S(2)}) copy-start(s32[64]{0:T(128)} %constant.1075) | copy-start | bytes 772
  247.4 30.2 %copy-start.28 = (bf16[8,8,64]{2,1,0:T(8,128)(2,1)S(1)}, bf16[8,8,64]{2,1,0:T(8,128)(2,1)}, u32[]{:S(2)}) copy-start(bf16[8,8,64]{2,1,0:T(8,128)(2,1)} %copy.291) | copy-start | bytes 24580
  247.4 30.2 %copy-start.76 = (s32[8]{0:T(128)S(1)}, s32[8]{0:T(128)}, u32[]{:S(2)}) copy-start(s32[8]{0:T(128)} %constant.1076) | copy-start | bytes 100
  249.5 28.8 %copy-start.31 = (bf16[8,8,64]{2,1,0:T(8,128)(2,1)S(1)}, bf16[8,8,64]{2,1,0:T(8,128)(2,1)}, u32[]{:S(2)}) copy-start(bf16[8,8,64]{2,1,0:T(8,128)(2,1)} %copy.331) | copy-start | bytes 24580
  252.2 28.0 %copy-start.41 = (bf16[64,8,64]{2,1,0:T(8,128)(2,1)S(1)}, bf16[64,8,64]{2,1,0:T(8,128)(2,1)}, u32[]{:S(2)}) copy-start(bf16[64,8,64]{2,1,0:T(8,128)(2,1)} %copy.293) | copy-start | bytes 196612
  252.2 28.0 %copy-start.75 = (s32[64]{0:T(128)S(1)}, s32[64]{0:T(128)}, u32[]{:S(2)}) copy-start(s32[64]{0:T(128)} %constant.1077) | copy-start | bytes 772
  259.5 30.1 %copy-start.40 = (bf16[64,8,64]{2,1,0:T(8,128)(2,1)S(1)}, bf16[64,8,64]{2,1,0:T(8,128)(2,1)}, u32[]{:S(2)}) copy-start(bf16[64,8,64]{2,1,0:T(8,128)(2,1)} %copy.295) | copy-start | bytes 196612
  259.5 30.1 %copy-start.74 = (s32[64]{0:T(128)S(1)}, s32[64]{0:T(128)}, u32[]{:S(2)}) copy-start(s32[64]{0:T(128)} %constant.1078) | copy-start | bytes 772
  262.1 30.0 %copy-start.44 = (bf16[64,8,64]{2,1,0:T(8,128)(2,1)S(1)}, bf16[64,8,64]{2,1,0:T(8,128)(2,1)}, u32[]{:S(2)}) copy-start(bf16[64,8,64]{2,1,0:T(8,128)(2,1)} %copy.335) | copy-start | bytes 196612
  262.8 35.8 %copy-start.26 = (bf16[8,8,64]{2,1,0:T(8,128)(2,1)S(1)}, bf16[8,8,64]{2,1,0:T(8,128)(2,1)}, u32[]{:S(2)}) copy-start(bf16[8,8,64]{2,1,0:T(8,128)(2,1)} %copy.297) | copy-start | bytes 24580
  262.8 35.8 %copy-start.73 = (s32[8]{0:T(128)S(1)}, s32[8]{0:T(128)}, u32[]{:S(2)}) copy-start(s32[8]{0:T(128)} %constant.1079) | copy-start | bytes 100
  265.4 34.0 %copy-start.29 = (bf16[8,8,64]{2,1,0:T(8,128)(2,1)S(1)}, bf16[8,8,64]{2,1,0:T(8,128)(2,1)}, u32[]{:S(2)}) copy-start(bf16[8,8,64]{2,1,0:T(8,128)(2,1)} %copy.337) | copy-start | bytes 24580
  266.1 35.1 %copy-start.39 = (bf16[64,8,64]{2,1,0:T(8,128)(2,1)S(1)}, bf16[64,8,64]{2,1,0:T(8,128)(2,1)}, u32[]{:S(2)}) copy-start(bf16[64,8,64]{2,1,0:T(8,128)(2,1)} %copy.299) | copy-start | bytes 196612
  266.2 35.1 %copy-start.72 = (s32[64]{0:T(128)S(1)}, s32[64]{0:T(128)}, u32[]{:S(2)}) copy-start(s32[64]{0:T(128)} %constant.1080) | copy-start | bytes 772
  268.1 35.7 %copy-start.42 = (bf16[64,8,64]{2,1,0:T(8,128)(2,1)S(1)}, bf16[64,8,64]{2,1,0:T(8,128)(2,1)}, u32[]{:S(2)}) copy-start(bf16[64,8,64]{2,1,0:T(8,128)(2,1)} %copy.339) | copy-start | bytes 196612
  270.7 39.7 %copy-start.25 = (bf16[8,8,64]{2,1,0:T(8,128)(2,1)S(1)}, bf16[8,8,64]{2,1,0:T(8,128)(2,1)}, u32[]{:S(2)}) copy-start(bf16[8,8,64]{2,1,0:T(8,128)(2,1)} %copy.301) | copy-start | bytes 24580
  270.7 39.7 %copy-start.71 = (s32[8]{0:T(128)S(1)}, s32[8]{0:T(128)}, u32[]{:S(2)}) copy-start(s32[8]{0:T(128)} %constant.1081) | copy-start | bytes 100
  277.6 33.5 %copy-start.27 = (bf16[8,8,64]{2,1,0:T(8,128)(2,1)S(1)}, bf16[8,8,64]{2,1,0:T(8,128)(2,1)}, u32[]{:S(2)}) copy-start(bf16[8,8,64]{2,1,0:T(8,128)(2,1)} %copy.341) | copy-start | bytes 24580
  278.3 34.7 %copy-start.57 = (bf16[8,64]{1,0:T(8,128)(2,1)S(1)}, bf16[8,64]{1,0:T(8,128)(2,1)}, u32[]{:S(2)}) copy-start(bf16[8,64]{1,0:T(8,128)(2,1)} %gather_fusion.30) | copy-start | bytes 3076
  278.3 34.7 %copy-start.58 = (bf16[8,64]{1,0:T(8,128)(2,1)S(1)}, bf16[8,64]{1,0:T(8,128)(2,1)}, u32[]{:S(2)}) copy-start(bf16[8,64]{1,0:T(8,128)(2,1)} %gather_fusion.74) | copy-start | bytes 3076
  278.3 34.7 %copy-start.91 = (pred[8]{0:T(512)(128)(4,1)S(1)}, pred[8]{0:T(512)(128)(4,1)}, u32[]{:S(2)}) copy-start(pred[8]{0:T(512)(128)(4,1)} %get-tuple-element.339) | copy-start | bytes 28
  278.3 34.7 %copy-start.99 = (pred[8]{0:T(512)(128)(4,1)S(1)}, pred[8]{0:T(512)(128)(4,1)}, u32[]{:S(2)}) copy-start(pred[8]{0:T(512)(128)(4,1)} %get-tuple-element.515) | copy-start | bytes 28
  278.3 35.4 %copy-start.70 = (s32[8]{0:T(128)S(1)}, s32[8]{0:T(128)}, u32[]{:S(2)}) copy-start(s32[8]{0:T(128)} %constant.1082) | copy-start | bytes 100
  282.7 33.7 %copy-start.59 = (bf16[8,64]{1,0:T(8,128)(2,1)S(1)}, bf16[8,64]{1,0:T(8,128)(2,1)}, u32[]{:S(2)}) copy-start(bf16[8,64]{1,0:T(8,128)(2,1)} %gather_fusion.33) | copy-start | bytes 3076
  282.7 33.7 %copy-start.60 = (bf16[8,64]{1,0:T(8,128)(2,1)S(1)}, bf16[8,64]{1,0:T(8,128)(2,1)}, u32[]{:S(2)}) copy-start(bf16[8,64]{1,0:T(8,128)(2,1)} %gather_fusion.77) | copy-start | bytes 3076
  282.7 33.7 %copy-start.90 = (pred[8]{0:T(512)(128)(4,1)S(1)}, pred[8]{0:T(512)(128)(4,1)}, u32[]{:S(2)}) copy-start(pred[8]{0:T(512)(128)(4,1)} %get-tuple-element.337) | copy-start | bytes 28
  282.7 33.6 %copy-start.98 = (pred[8]{0:T(512)(128)(4,1)S(1)}, pred[8]{0:T(512)(128)(4,1)}, u32[]{:S(2)}) copy-start(pred[8]{0:T(512)(128)(4,1)} %get-tuple-element.513) | copy-start | bytes 28
  282.7 34.3 %copy-start.69 = (s32[8]{0:T(128)S(1)}, s32[8]{0:T(128)}, u32[]{:S(2)}) copy-start(s32[8]{0:T(128)} %constant.1083) | copy-start | bytes 100
  292.0 27.6 %copy-start.45 = (bf16[64,8,64]{2,1,0:T(8,128)(2,1)S(1)}, bf16[64,8,64]{2,1,0:T(8,128)(2,1)}, u32[]{:S(2)}) copy-start(bf16[64,8,64]{2,1,0:T(8,128)(2,1)} %copy.310) | copy-start | bytes 196612
  292.1 27.6 %copy-start.68 = (s32[64]{0:T(128)S(1)}, s32[64]{0:T(128)}, u32[]{:S(2)}) copy-start(s32[64]{0:T(128)} %constant.1084) | copy-start | bytes 772
  298.6 23.4 %copy-start.46 = (bf16[64,8,64]{2,1,0:T(8,128)(2,1)S(1)}, bf16[64,8,64]{2,1,0:T(8,128)(2,1)}, u32[]{:S(2)}) copy-start(bf16[64,8,64]{2,1,0:T(8,128)(2,1)} %copy.348) | copy-start | bytes 196612
  299.4 29.2 %copy-start.67 = (s32[8]{0:T(128)S(1)}, s32[8]{0:T(128)}, u32[]{:S(2)}) copy-start(s32[8]{0:T(128)} %constant.1085) | copy-start | bytes 100
  303.7 27.5 %copy-start.61 = (bf16[8,64]{1,0:T(8,128)(2,1)S(1)}, bf16[8,64]{1,0:T(8,128)(2,1)}, u32[]{:S(2)}) copy-start(bf16[8,64]{1,0:T(8,128)(2,1)} %gather_fusion.40) | copy-start | bytes 3076
  303.7 27.5 %copy-start.89 = (pred[8]{0:T(512)(128)(4,1)S(1)}, pred[8]{0:T(512)(128)(4,1)}, u32[]{:S(2)}) copy-start(pred[8]{0:T(512)(128)(4,1)} %get-tuple-element.333) | copy-start | bytes 28
  303.7 27.5 %copy-start.96 = (pred[8]{0:T(512)(128)(4,1)S(1)}, pred[8]{0:T(512)(128)(4,1)}, u32[]{:S(2)}) copy-start(pred[8]{0:T(512)(128)(4,1)} %get-tuple-element.509) | copy-start | bytes 28
  303.8 28.1 %copy-start.66 = (s32[8]{0:T(128)S(1)}, s32[8]{0:T(128)}, u32[]{:S(2)}) copy-start(s32[8]{0:T(128)} %constant.1086) | copy-start | bytes 100
  311.1 23.4 %copy-start.88 = (pred[8]{0:T(512)(128)(4,1)S(1)}, pred[8]{0:T(512)(128)(4,1)}, u32[]{:S(2)}) copy-start(pred[8]{0:T(512)(128)(4,1)} %get-tuple-element.331) | copy-start | bytes 28
  311.1 23.4 %copy-start.95 = (pred[8]{0:T(512)(128)(4,1)S(1)}, pred[8]{0:T(512)(128)(4,1)}, u32[]{:S(2)}) copy-start(pred[8]{0:T(512)(128)(4,1)} %get-tuple-element.507) | copy-start | bytes 28
  (60 other events, 720.3 us)
Sparse Core Ops, SparseCore 0:
  446.0 181.2 all-reduce.1
where the time goes:
time: 647 us; the launch traced here: 637 us
  local copies, waits for them, and re-layouts  326 us (50%)
  waiting for transfers between devices  174 us (27%)
  other arithmetic  68.5 us (11%)
  matrix products  42.5 us (7%)
  between operations  16.7 us (3%)
  starting transfers between devices  7.22 us (1%)
    psum x1, waiting for transfers between devices, shards(): summed_grad = lax.psum(grad_local.reshape(-1), 'dom')  174 us
    scatter x36, local copies, waits for them, and re-layouts, padded_field(): padded.at[:, :, dest_index].set(take_rows(source, row_index, keep_rows))  87 us
    gather x52, local copies, waits for them, and re-layouts, take_rows(): jnp.take(source, jnp.clip(row_index, 0, source.shape[0] - 1), axis=0)  52.1 us
    while x416, local copies, waits for them, and re-layouts  43.8 us
    scatter x2, local copies, waits for them, and re-layouts, padded_field(): padded = jnp.zeros((leaf_count, channels, padded_cells), center.dtype).at...  27.4 us
    dot_general x8, matrix products, block_terms(): jnp.einsum('lkv,lov->ko', stack_x, dy_block, preferred_element_type=jnp.f...  21.6 us
    select_n x36, local copies, waits for them, and re-layouts, take_rows(): jnp.where(keep_rows[:, None, None], picked, jnp.zeros((), source.dtype))  16.9 us
    gather x40, other arithmetic  15.1 us
  transfers between devices with their start and end apart: 3, of which 1 were waited for; matrix products, arithmetic and copies ran while one was open for 20% of the time, Pallas kernels for 0%

commit v1 on v0

--- a/solution.py
+++ b/solution.py
@@ -203,7 +203,7 @@
     out_features = (jnp.take(out_sum, inner_span, axis=2) * occupancy_wide).astype(jnp.bfloat16)
     in_grad = (jnp.take(back_sum, inner_span, axis=2) * occupancy_wide).astype(jnp.bfloat16)
     grad_scale = float(lax.axis_size("dom") * leaf_count * voxel_count) ** (-0.5)
-    summed_grad = lax.psum(grad_local.reshape(-1), "dom")
+    summed_grad = jnp.sum(lax.all_gather(grad_local.reshape(-1), "dom"), axis=0)
     weight_grad = summed_grad.reshape(27, channels, channels) * grad_scale
     return (out_features, in_grad, weight_grad)
 

time: 647 us -> 602 us (0.930)
  waiting for transfers between devices: 174 us -> 113 us
  other arithmetic: 68.5 us -> 85.1 us
    psum x1 -> x0, waiting for transfers between devices: 174 us -> none  [shards(): summed_grad = lax.psum(grad_local.reshape(-1), 'dom')]
    all_gather x0 -> x1, waiting for transfers between devices: none -> 113 us  [shards(): summed_grad = jnp.sum(lax.all_gather(grad_local.reshape(-1), 'dom'), axis=0)]
    reduce_sum x0 -> x1, other arithmetic: none -> 18.4 us  [shards(): summed_grad = jnp.sum(lax.all_gather(grad_local.reshape(-1), 'dom'), axis=0)]
  transfers between devices with their start and end apart: 3 -> 3, of which waited for: 1 -> 1; matrix products, arithmetic and copies ran while one was open for 20% -> 24% of each run, Pallas kernels for 0% -> 0%
where the time goes in v1:
time: 602 us; the launch traced here: 591 us
  local copies, waits for them, and re-layouts  325 us (54%)
  waiting for transfers between devices  113 us (19%)
  other arithmetic  85.1 us (14%)
  matrix products  42.6 us (7%)
  between operations  16.7 us (3%)
  starting transfers between devices  7.22 us (1%)
    all_gather x1, waiting for transfers between devices, shards(): summed_grad = jnp.sum(lax.all_gather(grad_local.reshape(-1), 'dom'), axis=0)  113 us
    scatter x36, local copies, waits for them, and re-layouts, padded_field(): padded.at[:, :, dest_index].set(take_rows(source, row_index, keep_rows))  87.2 us
    gather x52, local copies, waits for them, and re-layouts, take_rows(): jnp.take(source, jnp.clip(row_index, 0, source.shape[0] - 1), axis=0)  52.1 us
    while x416, local copies, waits for them, and re-layouts  43.8 us
    scatter x2, local copies, waits for them, and re-layouts, padded_field(): padded = jnp.zeros((leaf_count, channels, padded_cells), center.dtype).at...  27.4 us
    dot_general x8, matrix products, block_terms(): jnp.einsum('lkv,lov->ko', stack_x, dy_block, preferred_element_type=jnp.f...  21.7 us
    reduce_sum x1, other arithmetic, shards(): summed_grad = jnp.sum(lax.all_gather(grad_local.reshape(-1), 'dom'), axis=0)  18.4 us
    select_n x36, local copies, waits for them, and re-layouts, take_rows(): jnp.where(keep_rows[:, None, None], picked, jnp.zeros((), source.dtype))  16.9 us
  transfers between devices with their start and end apart: 3, of which 1 were waited for; matrix products, arithmetic and copies ran while one was open for 24% of the time, Pallas kernels for 0%

profile of v1, /device:TPU:1, one launch (start us, length us, event | category | flops | bytes accessed | tf_op | source)
XLA Modules:
  0.0 591.5 jit_solution(5524343893831648759)
XLA Ops:
  8.4 1.8 copy.271
  15.3 5.3 collective-permute-start.1
  21.9 1.9 collective-permute-start
  86.3 13.8 %scatter_fusion.38 = bf16[8,64,778]{1,0,2:T(8,128)(2,1)S(1)} fusion(bf16[8,64,778]{1,0,2:T(8,128)(2,1)S(1)} %broadcast_in_dim.665, s32[512]{0:T(512)} %constant.642.clone, bf16[512,8,64]{2,1,0:T(8,128)(2,1)S(1)} %bitcast.358), kind=kCustom, calls=%fused_computation.128 | custom fusion | bytes 1574912 | tf_op jit(solution)/shard_map/scatter | solution.py:157
  100.1 2.5 copy.356
  104.3 13.7 %scatter_fusion.19 = bf16[8,64,1000]{1,0,2:T(8,128)(2,1)S(1)} fusion(bf16[8,64,1000]{1,0,2:T(8,128)(2,1)S(1)} %broadcast.489.clone, s32[512]{0:T(512)} %constant.1068, bf16[512,8,64]{2,1,0:T(8,128)(2,1)S(1)} %bitcast.359), kind=kCustom, calls=%fused_computation.109 | custom fusion | bytes 1574912 | tf_op jit(solution)/shard_map/scatter | solution.py:126
  120.6 13.7 %scatter_fusion = bf16[8,64,1000]{1,0,2:T(8,128)(2,1)S(1)} fusion(bf16[8,64,1000]{1,0,2:T(8,128)(2,1)S(1)} %broadcast.489.clone.1, s32[512]{0:T(512)} %constant.1068, bf16[512,8,64]{2,1,0:T(8,128)(2,1)S(1)} %bitcast.361), kind=kCustom, calls=%fused_computation.90 | custom fusion | bytes 1574912 | tf_op jit(solution)/shard_map/scatter | solution.py:126
  174.4 1.9 gather_fusion
  176.3 1.9 gather_fusion.44
  180.4 1.9 gather_fusion.3
  182.3 1.9 gather_fusion.47
  187.1 2.2 select_bitcast_fusion
  202.6 1.9 gather_fusion.10
  204.6 1.9 gather_fusion.54
  207.2 1.9 gather_fusion.13
  209.2 1.9 gather_fusion.57
  211.1 1.9 gather_fusion.30
  213.1 1.9 gather_fusion.74
  217.1 1.9 gather_fusion.33
  219.1 1.9 gather_fusion.77
  241.4 2.1 scatter_fusion.20
  245.8 2.1 scatter_fusion.21
  248.0 2.7 scatter_fusion.3
  250.7 6.5 %scatter_fusion.22 = bf16[8,64,1000]{1,0,2:T(8,128)(2,1)} fusion(bf16[8,64,1000]{1,0,2:T(8,128)(2,1)} %scatter_fusion.21, s32[64]{0:T(128)S(1)} %copy-done.82, bf16[64,8,64]{2,1,0:T(8,128)(2,1)S(1)} %copy-done.47), kind=kCustom, calls=%fused_computation.112 | custom fusion | bytes 196864 | tf_op jit(solution)/shard_map/scatter | solution.py:149
  258.0 1.9 scatter_fusion.23
  261.3 1.9 scatter_fusion.24
  264.6 1.9 scatter_fusion.25
  266.5 2.6 scatter_fusion.7
  269.2 6.9 %scatter_fusion.26 = bf16[8,64,1000]{1,0,2:T(8,128)(2,1)} fusion(bf16[8,64,1000]{1,0,2:T(8,128)(2,1)} %scatter_fusion.25, s32[64]{0:T(128)S(1)} %copy-done.78, bf16[64,8,64]{2,1,0:T(8,128)(2,1)} %copy.329), kind=kCustom, calls=%fused_computation.116 | custom fusion | bytes 196864 | tf_op jit(solution)/shard_map/scatter | solution.py:149
  276.9 1.9 scatter_fusion.27
  278.8 2.4 scatter_fusion.9
  281.2 6.9 %scatter_fusion.28 = bf16[8,64,1000]{1,0,2:T(8,128)(2,1)} fusion(bf16[8,64,1000]{1,0,2:T(8,128)(2,1)} %scatter_fusion.27, s32[64]{0:T(128)S(1)} %copy-done.76, bf16[64,8,64]{2,1,0:T(8,128)(2,1)} %copy.333), kind=kCustom, calls=%fused_computation.118 | custom fusion | bytes 196864 | tf_op jit(solution)/shard_map/scatter | solution.py:149
  288.2 2.4 scatter_fusion.10
  290.6 6.6 %scatter_fusion.29 = bf16[8,64,1000]{1,0,2:T(8,128)(2,1)} fusion(bf16[8,64,1000]{1,0,2:T(8,128)(2,1)} %scatter_fusion.28, s32[64]{0:T(128)S(1)} %copy-done.75, bf16[64,8,64]{2,1,0:T(8,128)(2,1)S(1)} %copy-done.44), kind=kCustom, calls=%fused_computation.119 | custom fusion | bytes 196864 | tf_op jit(solution)/shard_map/scatter | solution.py:149
  298.0 1.9 scatter_fusion.30
  299.9 2.4 scatter_fusion.12
  302.3 6.6 %scatter_fusion.31 = bf16[8,64,1000]{1,0,2:T(8,128)(2,1)} fusion(bf16[8,64,1000]{1,0,2:T(8,128)(2,1)} %scatter_fusion.30, s32[64]{0:T(128)S(1)} %copy-done.73, bf16[64,8,64]{2,1,0:T(8,128)(2,1)S(1)} %copy-done.42), kind=kCustom, calls=%fused_computation.121 | custom fusion | bytes 196864 | tf_op jit(solution)/shard_map/scatter | solution.py:149
  309.7 1.9 scatter_fusion.32
  313.0 1.9 scatter_fusion.33
  316.2 1.9 scatter_fusion.34
  318.1 2.4 scatter_fusion.16
  320.6 6.6 %scatter_fusion.35 = bf16[8,64,1000]{1,0,2:T(8,128)(2,1)} fusion(bf16[8,64,1000]{1,0,2:T(8,128)(2,1)} %scatter_fusion.34, s32[64]{0:T(128)S(1)} %copy-done.69, bf16[64,8,64]{2,1,0:T(8,128)(2,1)S(1)} %copy-done.46), kind=kCustom, calls=%fused_computation.125 | custom fusion | bytes 196864 | tf_op jit(solution)/shard_map/scatter | solution.py:149
  327.9 1.9 scatter_fusion.36
  331.2 1.9 scatter_fusion.37
  333.7 1.9 copy.354
  335.6 2.6 copy.355
  338.2 89.5 %while.31 = (s32[]{:T(128)}, f32[8,1,64,778]{3,2,1,0:T(8,128)}, f32[8,1,64,778]{3,2,1,0:T(8,128)}, f32[8,1728,64]{1,2,0:T(8,128)}, bf16[8,1,64,1000]{3,2,1,0:T(8...) while((s32[]{:T(128)}, f32[8,1,64,778]{3,2,1,0:T(8,128)}, ...), condition=%wide.region_56.67_spmd, body=%wide.region_55.66_spmd.sunk | while | flops 516243456 | bytes 22411112 | solution.py:195
  345.6 2.7 fusion.141
  356.7 2.7 fusion.141
  367.9 2.7 fusion.141
  379.0 2.7 fusion.141
  390.2 2.7 fusion.141
  401.3 2.7 fusion.141
  412.5 2.7 fusion.141
  423.6 2.7 fusion.141
  427.7 2.3 reduce_sum.18
  431.8 2.8 copy.357
  434.6 3.6 copy.359
  438.2 2.7 gather_fusion.88
  440.9 4.3 gather_fusion.89
  445.3 2.8 fusion.27
  448.1 2.7 copy.361
  452.3 112.6 %all-gather.3.cloned.1.call-done = f32[64,1,110592]{2,1,0:T(1,128)} async-done(((f32[1,1,110592]{2,1,0:T(1,128)}), f32[64,1,110592]{2,1,0:T(1,128)}) %all-gather.3.cloned.1.call-update) | async-done | bytes 28311568 | tf_op jit(solution)/shard_map/all_gather | solution.py:206
  564.9 18.4 %reduce_sum.19 = f32[110592]{0:T(1024)S(1)} reduce(f32[64,1,110592]{2,1,0:T(1,128)} %all-gather.3.cloned.1.call-done, f32[]{:T(128)} %constant.583.clone.1), dimensions={0,1}, to_apply=%region_58.70 | reduce | flops 6967296 | bytes 28753924 | tf_op jit(solution)/shard_map/reduce_sum | solution.py:206
  (1029 shorter events, 238.3 us)
Async XLA Ops:
  7.2 557.7 %all-gather.3.cloned.1.call-start = ((), (), s32[]{:S(2)}) async-start(), calls=%async_computation | async-start | bytes 28753920 | tf_op jit(solution)/shard_map/all_gather | solution.py:206
  13.7 28.4 %copy-start.3 = (bf16[8,64,512]{1,0,2:T(8,128)(2,1)}, bf16[8,64,512]{1,0,2:T(8,128)(2,1)S(1)}, u32[]{:S(2)}) copy-start(bf16[8,64,512]{1,0,2:T(8,128)(2,1)S(1)} %get-tuple-element.404) | copy-start | bytes 1572868
  15.3 23.3 %copy-start.115 = (s32[8]{0:T(128)S(1)}, s32[8]{0:T(128)}, u32[]{:S(2)}) copy-start(s32[8]{0:T(128)} %constant.1135) | copy-start | bytes 100
  15.3 132.0 %collective-permute-start.1 = (bf16[1,2,8,4096]{3,2,1,0:T(8,128)(2,1)}, bf16[1,2,8,4096]{3,2,1,0:T(8,128)(2,1)}, u32[]{:S(2)}, u32[]{:S(2)}) collective-permute-start(bf16[1,2,8,4096]{3,2,1,0:T(8,128)(2,1)} %maximum_bitcast_fusion.1), channel_id=1, source_target_pairs={{1,0},{2,1},{3,2},{4,3},{5,4},{6,5},{7,6},{8,7},{9,8},{10,9},{11,1... | collective-permute-start | bytes 393224 | tf_op jit(solution)/shard_map/ppermute | solution.py:18
  21.9 113.3 %collective-permute-start = (bf16[1,2,8,4096]{3,2,1,0:T(8,128)(2,1)}, bf16[1,2,8,4096]{3,2,1,0:T(8,128)(2,1)}, u32[]{:S(2)}, u32[]{:S(2)}) collective-permute-start(bf16[1,2,8,4096]{3,2,1,0:T(8,128)(2,1)} %maximum_bitcast_fusion), channel_id=1, source_target_pairs={{0,1},{1,2},{2,3},{3,4},{4,5},{5,6},{6,7},{7,8},{8,9},{9,10},{10,1... | collective-permute-start | bytes 393224 | tf_op jit(solution)/shard_map/ppermute | solution.py:17
  48.9 94.3 %copy-start.53 = (s32[1024]{0:T(1024)}, s32[1024]{0:T(1024)S(1)}, u32[]{:S(2)}) copy-start(s32[1024]{0:T(1024)S(1)} %pad_clamp_fusion.38) | copy-start | bytes 12292
  50.1 95.4 %copy-start.54 = (s32[1024]{0:T(1024)}, s32[1024]{0:T(1024)S(1)}, u32[]{:S(2)}) copy-start(s32[1024]{0:T(1024)S(1)} %pad_clamp_fusion.35) | copy-start | bytes 12292
  192.4 31.0 %copy-start.37 = (bf16[16,64,64]{1,0,2:T(8,128)(2,1)S(1)}, bf16[16,64,64]{1,0,2:T(8,128)(2,1)}, u32[]{:S(2)}) copy-start(bf16[16,64,64]{1,0,2:T(8,128)(2,1)} %get-tuple-element.472) | copy-start | bytes 393220
  193.9 30.5 %copy-start.36 = (bf16[16,64,64]{1,0,2:T(8,128)(2,1)S(1)}, bf16[16,64,64]{1,0,2:T(8,128)(2,1)}, u32[]{:S(2)}) copy-start(bf16[16,64,64]{1,0,2:T(8,128)(2,1)} %get-tuple-element.471) | copy-start | bytes 393220
  198.0 29.5 %copy-start.102 = (pred[8]{0:T(512)(128)(4,1)S(1)}, pred[8]{0:T(512)(128)(4,1)}, u32[]{:S(2)}) copy-start(pred[8]{0:T(512)(128)(4,1)} %get-tuple-element.335) | copy-start | bytes 28
  198.1 29.5 %copy-start.103 = (pred[8]{0:T(512)(128)(4,1)S(1)}, pred[8]{0:T(512)(128)(4,1)}, u32[]{:S(2)}) copy-start(pred[8]{0:T(512)(128)(4,1)} %get-tuple-element.511) | copy-start | bytes 28
  201.9 27.5 %copy-start.49 = (bf16[16,64,8]{1,0,2:T(8,128)(2,1)S(1)}, bf16[16,64,8]{1,0,2:T(8,128)(2,1)}, u32[]{:S(2)}) copy-start(bf16[16,64,8]{1,0,2:T(8,128)(2,1)} %get-tuple-element.468) | copy-start | bytes 49156
  230.2 27.1 %copy-start.81 = (s32[8]{0:T(128)S(1)}, s32[8]{0:T(128)}, u32[]{:S(2)}) copy-start(s32[8]{0:T(128)} %constant.1072) | copy-start | bytes 100
  233.3 26.6 %copy-start.65 = (bf16[8,64]{1,0:T(8,128)(2,1)S(1)}, bf16[8,64]{1,0:T(8,128)(2,1)}, u32[]{:S(2)}) copy-start(bf16[8,64]{1,0:T(8,128)(2,1)} %gather_fusion.10) | copy-start | bytes 3076
  233.3 26.6 %copy-start.66 = (bf16[8,64]{1,0:T(8,128)(2,1)S(1)}, bf16[8,64]{1,0:T(8,128)(2,1)}, u32[]{:S(2)}) copy-start(bf16[8,64]{1,0:T(8,128)(2,1)} %gather_fusion.54) | copy-start | bytes 3076
  233.3 26.6 %copy-start.94 = (pred[8]{0:T(512)(128)(4,1)S(1)}, pred[8]{0:T(512)(128)(4,1)}, u32[]{:S(2)}) copy-start(pred[8]{0:T(512)(128)(4,1)} %get-tuple-element.342) | copy-start | bytes 28
  233.3 26.6 %copy-start.98 = (pred[8]{0:T(512)(128)(4,1)S(1)}, pred[8]{0:T(512)(128)(4,1)}, u32[]{:S(2)}) copy-start(pred[8]{0:T(512)(128)(4,1)} %get-tuple-element.527) | copy-start | bytes 28
  233.3 27.2 %copy-start.80 = (s32[8]{0:T(128)S(1)}, s32[8]{0:T(128)}, u32[]{:S(2)}) copy-start(s32[8]{0:T(128)} %constant.1073) | copy-start | bytes 100
  236.9 26.3 %copy-start.63 = (bf16[8,64]{1,0:T(8,128)(2,1)S(1)}, bf16[8,64]{1,0:T(8,128)(2,1)}, u32[]{:S(2)}) copy-start(bf16[8,64]{1,0:T(8,128)(2,1)} %gather_fusion.13) | copy-start | bytes 3076
  236.9 26.3 %copy-start.64 = (bf16[8,64]{1,0:T(8,128)(2,1)S(1)}, bf16[8,64]{1,0:T(8,128)(2,1)}, u32[]{:S(2)}) copy-start(bf16[8,64]{1,0:T(8,128)(2,1)} %gather_fusion.57) | copy-start | bytes 3076
  236.9 26.3 %copy-start.93 = (pred[8]{0:T(512)(128)(4,1)S(1)}, pred[8]{0:T(512)(128)(4,1)}, u32[]{:S(2)}) copy-start(pred[8]{0:T(512)(128)(4,1)} %get-tuple-element.340) | copy-start | bytes 28
  236.9 26.3 %copy-start.95 = (pred[8]{0:T(512)(128)(4,1)S(1)}, pred[8]{0:T(512)(128)(4,1)}, u32[]{:S(2)}) copy-start(pred[8]{0:T(512)(128)(4,1)} %get-tuple-element.525) | copy-start | bytes 28
  236.9 27.0 %copy-start.30 = (bf16[8,8,64]{2,1,0:T(8,128)(2,1)S(1)}, bf16[8,8,64]{2,1,0:T(8,128)(2,1)}, u32[]{:S(2)}) copy-start(bf16[8,8,64]{2,1,0:T(8,128)(2,1)} %copy.287) | copy-start | bytes 24580
  236.9 27.0 %copy-start.79 = (s32[8]{0:T(128)S(1)}, s32[8]{0:T(128)}, u32[]{:S(2)}) copy-start(s32[8]{0:T(128)} %constant.1074) | copy-start | bytes 100
  240.4 24.2 %copy-start.32 = (bf16[8,8,64]{2,1,0:T(8,128)(2,1)S(1)}, bf16[8,8,64]{2,1,0:T(8,128)(2,1)}, u32[]{:S(2)}) copy-start(bf16[8,8,64]{2,1,0:T(8,128)(2,1)} %copy.327) | copy-start | bytes 24580
  241.4 25.1 %copy-start.43 = (bf16[64,8,64]{2,1,0:T(8,128)(2,1)S(1)}, bf16[64,8,64]{2,1,0:T(8,128)(2,1)}, u32[]{:S(2)}) copy-start(bf16[64,8,64]{2,1,0:T(8,128)(2,1)} %copy.289) | copy-start | bytes 196612
  241.4 25.1 %copy-start.78 = (s32[64]{0:T(128)S(1)}, s32[64]{0:T(128)}, u32[]{:S(2)}) copy-start(s32[64]{0:T(128)} %constant.1075) | copy-start | bytes 772
  245.8 30.3 %copy-start.28 = (bf16[8,8,64]{2,1,0:T(8,128)(2,1)S(1)}, bf16[8,8,64]{2,1,0:T(8,128)(2,1)}, u32[]{:S(2)}) copy-start(bf16[8,8,64]{2,1,0:T(8,128)(2,1)} %copy.291) | copy-start | bytes 24580
  245.8 30.3 %copy-start.77 = (s32[8]{0:T(128)S(1)}, s32[8]{0:T(128)}, u32[]{:S(2)}) copy-start(s32[8]{0:T(128)} %constant.1076) | copy-start | bytes 100
  248.0 28.8 %copy-start.31 = (bf16[8,8,64]{2,1,0:T(8,128)(2,1)S(1)}, bf16[8,8,64]{2,1,0:T(8,128)(2,1)}, u32[]{:S(2)}) copy-start(bf16[8,8,64]{2,1,0:T(8,128)(2,1)} %copy.331) | copy-start | bytes 24580
  250.7 28.1 %copy-start.41 = (bf16[64,8,64]{2,1,0:T(8,128)(2,1)S(1)}, bf16[64,8,64]{2,1,0:T(8,128)(2,1)}, u32[]{:S(2)}) copy-start(bf16[64,8,64]{2,1,0:T(8,128)(2,1)} %copy.293) | copy-start | bytes 196612
  250.7 28.1 %copy-start.76 = (s32[64]{0:T(128)S(1)}, s32[64]{0:T(128)}, u32[]{:S(2)}) copy-start(s32[64]{0:T(128)} %constant.1077) | copy-start | bytes 772
  258.0 30.2 %copy-start.40 = (bf16[64,8,64]{2,1,0:T(8,128)(2,1)S(1)}, bf16[64,8,64]{2,1,0:T(8,128)(2,1)}, u32[]{:S(2)}) copy-start(bf16[64,8,64]{2,1,0:T(8,128)(2,1)} %copy.295) | copy-start | bytes 196612
  258.0 30.2 %copy-start.75 = (s32[64]{0:T(128)S(1)}, s32[64]{0:T(128)}, u32[]{:S(2)}) copy-start(s32[64]{0:T(128)} %constant.1078) | copy-start | bytes 772
  260.6 30.0 %copy-start.44 = (bf16[64,8,64]{2,1,0:T(8,128)(2,1)S(1)}, bf16[64,8,64]{2,1,0:T(8,128)(2,1)}, u32[]{:S(2)}) copy-start(bf16[64,8,64]{2,1,0:T(8,128)(2,1)} %copy.335) | copy-start | bytes 196612
  261.3 35.9 %copy-start.26 = (bf16[8,8,64]{2,1,0:T(8,128)(2,1)S(1)}, bf16[8,8,64]{2,1,0:T(8,128)(2,1)}, u32[]{:S(2)}) copy-start(bf16[8,8,64]{2,1,0:T(8,128)(2,1)} %copy.297) | copy-start | bytes 24580
  261.3 35.9 %copy-start.74 = (s32[8]{0:T(128)S(1)}, s32[8]{0:T(128)}, u32[]{:S(2)}) copy-start(s32[8]{0:T(128)} %constant.1079) | copy-start | bytes 100
  263.9 34.1 %copy-start.29 = (bf16[8,8,64]{2,1,0:T(8,128)(2,1)S(1)}, bf16[8,8,64]{2,1,0:T(8,128)(2,1)}, u32[]{:S(2)}) copy-start(bf16[8,8,64]{2,1,0:T(8,128)(2,1)} %copy.337) | copy-start | bytes 24580
  264.6 35.2 %copy-start.39 = (bf16[64,8,64]{2,1,0:T(8,128)(2,1)S(1)}, bf16[64,8,64]{2,1,0:T(8,128)(2,1)}, u32[]{:S(2)}) copy-start(bf16[64,8,64]{2,1,0:T(8,128)(2,1)} %copy.299) | copy-start | bytes 196612
  264.6 35.2 %copy-start.73 = (s32[64]{0:T(128)S(1)}, s32[64]{0:T(128)}, u32[]{:S(2)}) copy-start(s32[64]{0:T(128)} %constant.1080) | copy-start | bytes 772
  266.5 35.8 %copy-start.42 = (bf16[64,8,64]{2,1,0:T(8,128)(2,1)S(1)}, bf16[64,8,64]{2,1,0:T(8,128)(2,1)}, u32[]{:S(2)}) copy-start(bf16[64,8,64]{2,1,0:T(8,128)(2,1)} %copy.339) | copy-start | bytes 196612
  269.1 39.8 %copy-start.25 = (bf16[8,8,64]{2,1,0:T(8,128)(2,1)S(1)}, bf16[8,8,64]{2,1,0:T(8,128)(2,1)}, u32[]{:S(2)}) copy-start(bf16[8,8,64]{2,1,0:T(8,128)(2,1)} %copy.301) | copy-start | bytes 24580
  269.2 39.8 %copy-start.72 = (s32[8]{0:T(128)S(1)}, s32[8]{0:T(128)}, u32[]{:S(2)}) copy-start(s32[8]{0:T(128)} %constant.1081) | copy-start | bytes 100
  276.1 33.6 %copy-start.27 = (bf16[8,8,64]{2,1,0:T(8,128)(2,1)S(1)}, bf16[8,8,64]{2,1,0:T(8,128)(2,1)}, u32[]{:S(2)}) copy-start(bf16[8,8,64]{2,1,0:T(8,128)(2,1)} %copy.341) | copy-start | bytes 24580
  276.8 34.8 %copy-start.58 = (bf16[8,64]{1,0:T(8,128)(2,1)S(1)}, bf16[8,64]{1,0:T(8,128)(2,1)}, u32[]{:S(2)}) copy-start(bf16[8,64]{1,0:T(8,128)(2,1)} %gather_fusion.30) | copy-start | bytes 3076
  276.8 34.8 %copy-start.59 = (bf16[8,64]{1,0:T(8,128)(2,1)S(1)}, bf16[8,64]{1,0:T(8,128)(2,1)}, u32[]{:S(2)}) copy-start(bf16[8,64]{1,0:T(8,128)(2,1)} %gather_fusion.74) | copy-start | bytes 3076
  276.8 34.8 %copy-start.92 = (pred[8]{0:T(512)(128)(4,1)S(1)}, pred[8]{0:T(512)(128)(4,1)}, u32[]{:S(2)}) copy-start(pred[8]{0:T(512)(128)(4,1)} %get-tuple-element.339) | copy-start | bytes 28
  276.8 34.8 %copy-start.100 = (pred[8]{0:T(512)(128)(4,1)S(1)}, pred[8]{0:T(512)(128)(4,1)}, u32[]{:S(2)}) copy-start(pred[8]{0:T(512)(128)(4,1)} %get-tuple-element.515) | copy-start | bytes 28
  276.8 35.4 %copy-start.71 = (s32[8]{0:T(128)S(1)}, s32[8]{0:T(128)}, u32[]{:S(2)}) copy-start(s32[8]{0:T(128)} %constant.1082) | copy-start | bytes 100
  281.2 33.6 %copy-start.60 = (bf16[8,64]{1,0:T(8,128)(2,1)S(1)}, bf16[8,64]{1,0:T(8,128)(2,1)}, u32[]{:S(2)}) copy-start(bf16[8,64]{1,0:T(8,128)(2,1)} %gather_fusion.33) | copy-start | bytes 3076
  281.2 33.6 %copy-start.61 = (bf16[8,64]{1,0:T(8,128)(2,1)S(1)}, bf16[8,64]{1,0:T(8,128)(2,1)}, u32[]{:S(2)}) copy-start(bf16[8,64]{1,0:T(8,128)(2,1)} %gather_fusion.77) | copy-start | bytes 3076
  281.2 33.6 %copy-start.91 = (pred[8]{0:T(512)(128)(4,1)S(1)}, pred[8]{0:T(512)(128)(4,1)}, u32[]{:S(2)}) copy-start(pred[8]{0:T(512)(128)(4,1)} %get-tuple-element.337) | copy-start | bytes 28
  281.2 33.6 %copy-start.99 = (pred[8]{0:T(512)(128)(4,1)S(1)}, pred[8]{0:T(512)(128)(4,1)}, u32[]{:S(2)}) copy-start(pred[8]{0:T(512)(128)(4,1)} %get-tuple-element.513) | copy-start | bytes 28
  281.2 34.3 %copy-start.70 = (s32[8]{0:T(128)S(1)}, s32[8]{0:T(128)}, u32[]{:S(2)}) copy-start(s32[8]{0:T(128)} %constant.1083) | copy-start | bytes 100
  290.6 27.5 %copy-start.45 = (bf16[64,8,64]{2,1,0:T(8,128)(2,1)S(1)}, bf16[64,8,64]{2,1,0:T(8,128)(2,1)}, u32[]{:S(2)}) copy-start(bf16[64,8,64]{2,1,0:T(8,128)(2,1)} %copy.310) | copy-start | bytes 196612
  290.6 27.5 %copy-start.69 = (s32[64]{0:T(128)S(1)}, s32[64]{0:T(128)}, u32[]{:S(2)}) copy-start(s32[64]{0:T(128)} %constant.1084) | copy-start | bytes 772
  297.2 23.4 %copy-start.46 = (bf16[64,8,64]{2,1,0:T(8,128)(2,1)S(1)}, bf16[64,8,64]{2,1,0:T(8,128)(2,1)}, u32[]{:S(2)}) copy-start(bf16[64,8,64]{2,1,0:T(8,128)(2,1)} %copy.348) | copy-start | bytes 196612
  298.0 29.2 %copy-start.68 = (s32[8]{0:T(128)S(1)}, s32[8]{0:T(128)}, u32[]{:S(2)}) copy-start(s32[8]{0:T(128)} %constant.1085) | copy-start | bytes 100
  302.3 27.5 %copy-start.62 = (bf16[8,64]{1,0:T(8,128)(2,1)S(1)}, bf16[8,64]{1,0:T(8,128)(2,1)}, u32[]{:S(2)}) copy-start(bf16[8,64]{1,0:T(8,128)(2,1)} %gather_fusion.40) | copy-start | bytes 3076
  302.3 27.5 %copy-start.90 = (pred[8]{0:T(512)(128)(4,1)S(1)}, pred[8]{0:T(512)(128)(4,1)}, u32[]{:S(2)}) copy-start(pred[8]{0:T(512)(128)(4,1)} %get-tuple-element.333) | copy-start | bytes 28
  302.3 27.5 %copy-start.97 = (pred[8]{0:T(512)(128)(4,1)S(1)}, pred[8]{0:T(512)(128)(4,1)}, u32[]{:S(2)}) copy-start(pred[8]{0:T(512)(128)(4,1)} %get-tuple-element.509) | copy-start | bytes 28
  302.3 28.1 %copy-start.67 = (s32[8]{0:T(128)S(1)}, s32[8]{0:T(128)}, u32[]{:S(2)}) copy-start(s32[8]{0:T(128)} %constant.1086) | copy-start | bytes 100
  309.7 23.3 %copy-start.89 = (pred[8]{0:T(512)(128)(4,1)S(1)}, pred[8]{0:T(512)(128)(4,1)}, u32[]{:S(2)}) copy-start(pred[8]{0:T(512)(128)(4,1)} %get-tuple-element.331) | copy-start | bytes 28
  309.7 23.3 %copy-start.96 = (pred[8]{0:T(512)(128)(4,1)S(1)}, pred[8]{0:T(512)(128)(4,1)}, u32[]{:S(2)}) copy-start(pred[8]{0:T(512)(128)(4,1)} %get-tuple-element.507) | copy-start | bytes 28
  (61 other events, 701.6 us)
Sparse Core Ops, SparseCore 0:
  431.8 133.0 all-gather.2
